TPU v7x, 32 devices: a whole 2x2x4 slice. The times are simulated.
32 devices in a mesh: plane: 2 (over x), slab: 16 (over z, y, core).
Axes of the slice: x: 2, y: 2, z: 4, core: 2. Of those that a mesh axis runs over, the one named last changes fastest.
Arguments:
- kappa: float32 [2, 4096, 4096], P('plane', 'slab'), may hold values from -2.5 to 2.5
- ray_offsets: float32 [2, 16, 2, 32, 4096], P(None, 'slab', 'plane'), may hold values from -0.5 to 0.5
Outputs:
- deflection: float32 [2, 16, 2, 32, 4096], P(None, 'slab', 'plane')
- jacobian: float32 [4, 16, 2, 32, 4096], P(None, 'slab', 'plane')
All inputs are finite; a program needn't handle non-finite values.
Results may differ from a plain program's by a relative error of at most 0.0003.
Values sent between devices are 32-bit elements; how exact they have to be, the bound alone decides.
A program may use at most 128 MiB of HBM per device.

v0:
```python
import math

import jax
import jax.numpy as jnp
from jax import lax
from jax.sharding import PartitionSpec as P

STEP = 4
MARGIN = 8
PATCH_ROWS = 16
BLOCK = 64


lens_ratio = 0.5
screen_modes = 4.0


def factor_pair(length):
    outer = 1
    trial = 1
    while trial * trial <= length:
        if length % trial == 0:
            outer = trial
        trial = trial + 1
    return (outer, length // outer)


def cos_sin(left_ids, right_ids, length):
    angles = (left_ids[:, None] * right_ids[None, :] % length).astype(jnp.float32) * (
        2.0 * math.pi / length
    )
    return (jnp.cos(angles), jnp.sin(angles))


def contract_first(values, table):
    return jnp.einsum("...ab,ak->...kb", values, table, precision=lax.Precision.HIGHEST)


def contract_second(values, table):
    return jnp.einsum("...kb,bm->...mk", values, table, precision=lax.Precision.HIGHEST)


def transform_last(real_part, imag_part, sign):
    length = real_part.shape[-1]
    outer, inner = factor_pair(length)
    leading = real_part.shape[:-1]
    outer_ids = jnp.arange(outer, dtype=jnp.int32)
    inner_ids = jnp.arange(inner, dtype=jnp.int32)
    cos_outer, sin_outer = cos_sin(outer_ids, outer_ids, outer)
    cos_twist, sin_twist = cos_sin(outer_ids, inner_ids, length)
    cos_inner, sin_inner = cos_sin(inner_ids, inner_ids, inner)
    split_real = real_part.reshape(leading + (outer, inner))
    section_real = contract_first(split_real, cos_outer)
    section_imag = sign * contract_first(split_real, sin_outer)
    if imag_part is not None:
        split_imag = imag_part.reshape(leading + (outer, inner))
        section_real = section_real - sign * contract_first(split_imag, sin_outer)
        section_imag = section_imag + contract_first(split_imag, cos_outer)
    twist_real = section_real * cos_twist - sign * section_imag * sin_twist
    twist_imag = sign * section_real * sin_twist + section_imag * cos_twist
    final_real = contract_second(twist_real, cos_inner) - sign * contract_second(
        twist_imag, sin_inner
    )
    final_imag = sign * contract_second(twist_real, sin_inner) + contract_second(
        twist_imag, cos_inner
    )
    return (final_real.reshape(leading + (length,)), final_imag.reshape(leading + (length,)))


def wavenumbers(indices, length):
    folded = jnp.minimum(indices, length - indices).astype(jnp.float32)
    return 2.0 * math.pi / length * folded


def spline_terms(offset):
    magnitude = jnp.abs(offset)
    inside = magnitude < 1.0
    remain = jnp.maximum(2.0 - magnitude, 0.0)
    weights = jnp.where(
        inside,
        2.0 / 3.0 - magnitude * magnitude + 0.5 * magnitude * magnitude * magnitude,
        remain * remain * remain / 6.0,
    )
    slopes = jnp.sign(offset) * jnp.where(
        inside, -2.0 * magnitude + 1.5 * magnitude * magnitude, -0.5 * remain * remain
    )
    curves = jnp.where(inside, 3.0 * magnitude - 2.0, remain)
    return (weights, slopes, curves)


def lens_fields(plane_blocks, ycoord, xcoord):
    column_ids = jnp.arange(plane_blocks.shape[2]).astype(xcoord.dtype)
    row_ids = jnp.arange(plane_blocks.shape[0]).astype(ycoord.dtype)
    x_weights = jnp.stack(spline_terms(xcoord[:, :, None] - column_ids), axis=1)
    across = jnp.einsum("pbc,bkrc->bkpr", plane_blocks, x_weights, precision=lax.Precision.HIGHEST)
    down_weights, down_slopes, down_curves = spline_terms(ycoord[:, None, :] - row_ids[:, None])
    slope_down = jnp.sum(down_slopes * across[:, 0], axis=1)
    slope_across = jnp.sum(down_weights * across[:, 1], axis=1)
    bend_down = jnp.sum(down_curves * across[:, 0], axis=1)
    bend_across = jnp.sum(down_weights * across[:, 2], axis=1)
    bend_mixed = jnp.sum(down_slopes * across[:, 1], axis=1)
    return (slope_down, slope_across, bend_down, bend_across, bend_mixed)


def ray_row_outputs(window, shift_y, shift_x):
    grid_width = shift_y.shape[0]
    block_count = grid_width // BLOCK
    column_view = window.reshape(window.shape[0], PATCH_ROWS, block_count + 1, BLOCK)
    blocks = jnp.concatenate([column_view[:, :, :-1], column_view[:, :, 1:]], axis=3)
    centre_row = PATCH_ROWS // 2 - 1
    ycoord = centre_row + STEP * shift_y.reshape(block_count, BLOCK)
    xcoord = (
        BLOCK // 2 + jnp.arange(BLOCK).astype(shift_x.dtype) + shift_x.reshape(block_count, BLOCK)
    )
    first = lens_fields(blocks[0], ycoord, xcoord)
    second = lens_fields(blocks[1], ycoord - lens_ratio * first[0], xcoord - lens_ratio * first[1])
    hess_yy, hess_xx, hess_xy = (first[2], first[3], first[4])
    other_yy, other_xx, other_xy = (second[2], second[3], second[4])
    lensed_yy = 1.0 - lens_ratio * hess_yy
    lensed_xx = 1.0 - lens_ratio * hess_xx
    lensed_xy = -lens_ratio * hess_xy
    entry_yy = 1.0 - hess_yy - (other_yy * lensed_yy + other_xy * lensed_xy)
    entry_yx = -hess_xy - (other_yy * lensed_xy + other_xy * lensed_xx)
    entry_xy = -hess_xy - (other_xy * lensed_yy + other_xx * lensed_xy)
    entry_xx = 1.0 - hess_xx - (other_xy * lensed_xy + other_xx * lensed_xx)
    deflect = jnp.stack([first[0] + second[0], first[1] + second[1]]).reshape(2, grid_width)
    jacob = jnp.stack([entry_yy, entry_yx, entry_xy, entry_xx]).reshape(4, grid_width)
    return (deflect, jacob)


def on_device(kappa, ray_offsets):
    row_count = kappa.shape[1]
    grid_width = kappa.shape[2]
    slab_count = lax.axis_size("slab")
    plane_count = lax.axis_size("plane")
    half_rows = row_count // 2
    strip_rows = half_rows + 2 * MARGIN

    def to_local(values):
        return jnp.transpose(values.reshape(row_count, slab_count, row_count), (2, 1, 0)).reshape(
            row_count, grid_width
        )

    row_real, row_imag = transform_last(kappa[0], None, -1.0)
    recv_real, recv_imag = (
        lax.all_to_all(row_real, "slab", split_axis=1, concat_axis=1, tiled=True),
        lax.all_to_all(row_imag, "slab", split_axis=1, concat_axis=1, tiled=True),
    )
    spec_real, spec_imag = transform_last(to_local(recv_real), to_local(recv_imag), -1.0)
    first_wave = lax.axis_index("slab") * row_count
    wave_ids = jnp.arange(grid_width, dtype=jnp.int32)
    mine_ids = first_wave + jnp.arange(row_count, dtype=jnp.int32)
    wave_all = wavenumbers(wave_ids, grid_width)
    wave_mine = wavenumbers(mine_ids, grid_width)
    screen = (2.0 * math.pi * screen_modes / grid_width) ** 2
    denom = wave_mine[:, None] ** 2 + wave_all[None, :] ** 2 + screen
    anchor = (mine_ids[:, None] == 0) & (wave_ids[None, :] == 0)
    screened = jnp.where(anchor, 0.0, -2.0 / (denom * float(grid_width * grid_width)))
    inv_real, inv_imag = transform_last(spec_real * screened, spec_imag * screened, 1.0)

    def margined(values):
        middle = values.reshape(row_count, plane_count * slab_count, half_rows)
        upper = jnp.roll(middle[:, :, half_rows - MARGIN :], 1, axis=1)
        lower = jnp.roll(middle[:, :, :MARGIN], -1, axis=1)
        pieces = jnp.concatenate([upper, middle, lower], axis=2)
        pieces = jnp.transpose(
            pieces.reshape(row_count, slab_count, plane_count, strip_rows), (0, 2, 1, 3)
        )
        return pieces.reshape(row_count, plane_count * slab_count, strip_rows)

    arrived_real, arrived_imag = (
        lax.all_to_all(
            margined(inv_real), ("plane", "slab"), split_axis=1, concat_axis=1, tiled=True
        ),
        lax.all_to_all(
            margined(inv_imag), ("plane", "slab"), split_axis=1, concat_axis=1, tiled=True
        ),
    )

    def arrange(values):
        shaped = values.reshape(row_count, plane_count, slab_count, strip_rows)
        return jnp.transpose(shaped, (1, 3, 2, 0)).reshape(plane_count, strip_rows, grid_width)

    strips = transform_last(arrange(arrived_real), arrange(arrived_imag), 1.0)[0]
    padded = jnp.concatenate(
        [strips[:, :, grid_width - BLOCK // 2 :], strips, strips[:, :, : BLOCK // 2]], axis=2
    )
    ray_count = ray_offsets.shape[3]
    centre_row = PATCH_ROWS // 2 - 1
    row_shifts = ray_offsets[0, 0, 0]
    column_shifts = ray_offsets[1, 0, 0]

    def one_row(ray_row):
        first_row = STEP * ray_row + (STEP // 2 - centre_row + MARGIN)
        window = lax.dynamic_slice_in_dim(padded, first_row, PATCH_ROWS, 1)
        shift_y = lax.dynamic_index_in_dim(row_shifts, ray_row, 0, keepdims=False)
        shift_x = lax.dynamic_index_in_dim(column_shifts, ray_row, 0, keepdims=False)
        return ray_row_outputs(window, shift_y, shift_x)

    deflect, jacob = lax.map(one_row, jnp.arange(ray_count, dtype=jnp.int32))
    deflection = jnp.transpose(deflect, (1, 0, 2))[:, None, None]
    jacobian = jnp.transpose(jacob, (1, 0, 2))[:, None, None]
    return (deflection, jacobian)


def solution(mesh):
    placed = (P("plane", "slab", None), P(None, "slab", "plane", None, None))
    return jax.shard_map(
        on_device,
        mesh=mesh,
        in_specs=placed,
        out_specs=(P(None, "slab", "plane", None, None), P(None, "slab", "plane", None, None)),
        check_vma=False,
    )
```

profile of v0, /device:TPU:0, one launch (start us, length us, event | category | flops | bytes accessed | tf_op | source)
XLA Modules:
  0.0 2310.8 jit_solution(16082899711593844098)
XLA Ops:
  67.6 58.4 %all-to-all-done.1 = f32[256,16,256]{0,2,1:T(8,128)} async-done(((f32[256,16,256]{0,2,1:T(8,128)}), f32[256,16,256]{0,2,1:T(8,128)}, u32[]{:S(2)}, u32[]{:S(2)}) %all-to-all-start.1) | async-done | bytes 4194336 | tf_op jit(solution)/shard_map/all_to_all | solution.py:147
  126.0 19.9 all-to-all-start
  168.7 54.9 %all-to-all-done = f32[256,16,256]{0,2,1:T(8,128)} async-done(((f32[256,16,256]{0,2,1:T(8,128)}), f32[256,16,256]{0,2,1:T(8,128)}, u32[]{:S(2)}, u32[]{:S(2)}) %all-to-all-start) | async-done | bytes 4194336 | tf_op jit(solution)/shard_map/all_to_all | solution.py:146
  313.2 19.7 all-to-all-start.3
  353.1 85.7 %all-to-all-done.3 = f32[256,32,144]{0,2,1:T(8,128)} async-done(((f32[256,32,144]{0,2,1:T(8,128)}), f32[256,32,144]{0,2,1:T(8,128)}, u32[]{:S(2)}, u32[]{:S(2)}) %all-to-all-start.3) | async-done | bytes 4718624 | tf_op jit(solution)/shard_map/all_to_all | solution.py:175
  493.5 55.2 %all-to-all-done.2 = f32[256,32,144]{0,2,1:T(8,128)} async-done(((f32[256,32,144]{0,2,1:T(8,128)}), f32[256,32,144]{0,2,1:T(8,128)}, u32[]{:S(2)}, u32[]{:S(2)}) %all-to-all-start.2) | async-done | bytes 4718624 | tf_op jit(solution)/shard_map/all_to_all | solution.py:172
  588.2 19.5 subtract_bitcast_fusion.1
  607.8 15.9 fusion.102
  665.4 1645.2 %while.15 = (s32[]{:T(128)}, f32[32,2,4096]{2,0,1:T(8,128)}, f32[32,4,4096]{2,0,1:T(8,128)}, s32[32]{0:T(128)S(1)}, f32[32,4096]{1,0:T(8,128)}, /*index=5*/f32[3...) while((s32[]{:T(128)}, f32[32,2,4096]{2,0,1:T(8,128)}, ...), condition=%wide.region_11.12_spmd, body=%wide.region_0.11_spmd.sunk | while | flops 642666752 | bytes 59247396 | solution.py:200
  678.8 14.4 fusion.400
  730.2 14.4 fusion.400
  781.6 14.4 fusion.400
  833.0 14.4 fusion.400
  884.4 14.4 fusion.400
  935.8 14.4 fusion.400
  1038.6 14.4 fusion.400
  1090.1 14.4 fusion.400
  1141.5 14.4 fusion.400
  1192.9 14.4 fusion.400
  1244.3 14.4 fusion.400
  1295.7 14.4 fusion.400
  1347.1 14.4 fusion.400
  1398.5 14.4 fusion.400
  1449.9 14.4 fusion.400
  (1486 shorter events, 1685.5 us)
Async XLA Ops:
  40.5 85.5 %all-to-all-start.1 = ((f32[256,16,256]{0,2,1:T(8,128)}), f32[256,16,256]{0,2,1:T(8,128)}, u32[]{:S(2)}, u32[]{:S(2)}) async-start(f32[256,16,256]{0,2,1:T(8,128)} %bitcast.241), calls=%async_computation.1 | async-start | bytes 8388608 | tf_op jit(solution)/shard_map/all_to_all | solution.py:147
  126.0 97.5 %all-to-all-start = ((f32[256,16,256]{0,2,1:T(8,128)}), f32[256,16,256]{0,2,1:T(8,128)}, u32[]{:S(2)}, u32[]{:S(2)}) async-start(f32[256,16,256]{0,2,1:T(8,128)} %bitcast.240), calls=%async_computation | async-start | bytes 8388608 | tf_op jit(solution)/shard_map/all_to_all | solution.py:146
  313.2 125.5 %all-to-all-start.3 = ((f32[256,32,144]{0,2,1:T(8,128)}), f32[256,32,144]{0,2,1:T(8,128)}, u32[]{:S(2)}, u32[]{:S(2)}) async-start(f32[256,32,144]{0,2,1:T(8,128)} %bitcast.238), calls=%async_computation.3 | async-start | bytes 9437184 | tf_op jit(solution)/shard_map/all_to_all | solution.py:175
  438.7 110.0 %all-to-all-start.2 = ((f32[256,32,144]{0,2,1:T(8,128)}), f32[256,32,144]{0,2,1:T(8,128)}, u32[]{:S(2)}, u32[]{:S(2)}) async-start(f32[256,32,144]{0,2,1:T(8,128)} %bitcast.239), calls=%async_computation.2 | async-start | bytes 9437184 | tf_op jit(solution)/shard_map/all_to_all | solution.py:172
  607.8 15.9 copy-start.14
  678.8 14.4 copy-start.2
  730.2 14.4 copy-start.2
  833.0 14.4 copy-start.2
  884.4 14.4 copy-start.2
  935.8 14.4 copy-start.2
  987.2 14.4 copy-start.2
  1090.1 14.4 copy-start.2
  1192.9 14.4 copy-start.2
  1244.3 14.4 copy-start.2
  1295.7 14.4 copy-start.2
  1347.1 14.4 copy-start.2
  1449.9 14.4 copy-start.2
  1501.3 14.4 copy-start.2
  1552.7 14.4 copy-start.2
  1604.1 14.4 copy-start.2
  1655.5 14.4 copy-start.2
  1706.9 14.4 copy-start.2
  1809.8 14.4 copy-start.2
  1861.2 14.4 copy-start.2
  (121 other events, 564.3 us)
where the time goes:
time: 2320 us; the launch traced here: 2310 us
  matrix products  1120 us (48%)
  local copies, waits for them, and re-layouts  455 us (20%)
  other arithmetic  351 us (15%)
  waiting for transfers between devices  254 us (11%)
  loops' own time  79 us (3%)
  starting transfers between devices  51.5 us (2%)
    dot_general x64, matrix products, lens_fields(): jnp.einsum('pbc,bkrc->bkpr', plane_blocks, x_weights, precision=lax.Preci...  881 us
    select_n x64, other arithmetic, spline_terms(): jnp.where(inside, 2.0 / 3.0 - magnitude * magnitude + 0.5 * magnitude * m...  189 us
    dot_general x14, matrix products, contract_first(): jnp.einsum('...ab,ak->...kb', values, table, precision=lax.Precision.HIGH...  125 us
    dynamic_update_slice x128, local copies, waits for them, and re-layouts, on_device(): deflect, jacob = lax.map(one_row, jnp.arange(ray_count, dtype=jnp.int32))  120 us
    reduce_sum x64, other arithmetic, lens_fields(): bend_down = jnp.sum(down_curves * across[:, 0], axis=1)  120 us
    dot_general x14, matrix products, contract_second(): jnp.einsum('...kb,bm->...mk', values, table, precision=lax.Precision.HIGH...  113 us
    all_to_all x1, waiting for transfers between devices, on_device(): lax.all_to_all(margined(inv_imag), ('plane', 'slab'), split_axis=1, conca...  85.7 us
    another operation x1, loops' own time, on_device(): deflect, jacob = lax.map(one_row, jnp.arange(ray_count, dtype=jnp.int32))  79 us
  transfers between devices with their start and end apart: 4, of which 4 were waited for; matrix products, arithmetic and copies ran while one was open for 5% of the time, Pallas kernels for 0%

commit v1 on v0

v1 whole, which is shorter than its diff:
```python
import functools
import math

import jax
import jax.numpy as jnp
import ml_dtypes
import numpy as np
from jax import lax
from jax.experimental import pallas as pl
from jax.experimental.pallas import tpu as pltpu
from jax.sharding import PartitionSpec as P

STEP = 4
MARGIN = 8
PATCH_ROWS = 16
BLOCK = 64
RADIX = 16
LANES = 128
GROUP = 8

lens_ratio = 0.5
screen_modes = 4.0


def pair_residues():
    return [(0, RADIX // 2)] + [(r, RADIX - r) for r in range(1, RADIX // 2)]


def pair_tables(length):
    inner = length // RADIX
    n = np.arange(inner)[:, None]
    q = np.arange(inner)[None, :]
    tables = np.zeros((RADIX // 2, 2 * inner, 2 * inner))

    def angle(residue):
        return 2.0 * np.pi * (((RADIX * q + residue) * n) % length) / length

    for p, (first, second) in enumerate(pair_residues()):
        a, b = angle(first), angle(second)
        tables[p, :inner, :inner] = np.cos(a) + np.sin(a)
        if p == 0:
            tables[p, inner:, inner:] = np.cos(b) + np.sin(b)
        else:
            tables[p, inner:, :inner] = np.cos(a) - np.sin(a)
            tables[p, :inner, inner:] = np.cos(b) + np.sin(b)
            tables[p, inner:, inner:] = -(np.cos(b) - np.sin(b))
    return tables


def split_table(table, count):
    parts = []
    for _ in range(count):
        parts.append(table.astype(ml_dtypes.bfloat16))
        table = table - parts[-1].astype(np.float64)
    return np.stack(parts, axis=1)


def split(values, count):
    parts = []
    for _ in range(count):
        parts.append(values.astype(jnp.bfloat16))
        values = values - parts[-1].astype(jnp.float32)
    return parts


def split_dot(left, right, right_axis=0):
    total = None
    for order in range(len(left) - 1, -1, -1):
        for i in range(order + 1):
            term = lax.dot_general(
                left[i],
                right[order - i],
                (((1,), (right_axis,)), ((), ())),
                preferred_element_type=jnp.float32,
            )
            total = term if total is None else total + term
    return total


def weighted(terms):
    total = None
    for value, weight in terms:
        if abs(weight) < 1e-12:
            continue
        if abs(weight - 1.0) < 1e-12:
            total = value if total is None else total + value
        elif abs(weight + 1.0) < 1e-12:
            total = -value if total is None else total - value
        else:
            total = weight * value if total is None else total + weight * value
    return total


def cosine_sums(e):
    half = RADIX // 2
    quarter = half // 2
    fold = [e[i] + e[half - i] for i in range(quarter)] + [e[quarter]]
    diff = [e[i] - e[half - i] for i in range(quarter)]
    return [
        weighted(
            (v, math.cos(2.0 * math.pi * i * r / RADIX))
            for i, v in enumerate(fold if r % 2 == 0 else diff)
        )
        for r in range(half + 1)
    ]


def sine_sums(o):
    half = RADIX // 2
    quarter = half // 2
    odd = [None] + [o[i] + o[half - i] for i in range(1, quarter)] + [o[quarter]]
    even = [None] + [o[i] - o[half - i] for i in range(1, quarter)]
    sums = [None]
    for r in range(1, half):
        terms = odd if r % 2 == 1 else even
        sums.append(
            weighted(
                (terms[i], math.sin(2.0 * math.pi * i * r / RADIX)) for i in range(1, len(terms))
            )
        )
    return sums


def radix_forward(x):
    half = RADIX // 2
    e = [x[0]] + [x[i] + x[RADIX - i] for i in range(1, half)] + [x[half]]
    o = [None] + [x[i] - x[RADIX - i] for i in range(1, half)]
    c = cosine_sums(e)
    s = sine_sums(o)
    return [(c[0], c[half])] + [(c[r], s[r]) for r in range(1, half)]


def radix_inverse(pairs):
    half = RADIX // 2
    even = cosine_sums([pairs[0][0]] + [pairs[r][0] for r in range(1, half)] + [pairs[0][1]])
    odd = sine_sums([None] + [pairs[r][1] for r in range(1, half)])
    out = [None] * RADIX
    out[0], out[half] = even[0], even[half]
    for i in range(1, half):
        out[i] = even[i] + odd[i]
        out[RADIX - i] = even[i] - odd[i]
    return out


def lane_slices(width):
    size = min(width, LANES)
    return [(start, size) for start in range(0, width, size)]


def rows_forward_kernel(x_ref, table_ref, out_ref, high, low):
    rows, length = x_ref.shape
    inner = length // RADIX
    piece = out_ref.shape[2]

    @pl.when(pl.program_id(0) == 0)
    def _():
        def body(i, carry):
            here = pl.ds(pl.multiple_of(i * 16, 16), 16)
            for start, size in lane_slices(inner):
                chunks = [
                    x_ref[here, l * inner + start : l * inner + start + size] for l in range(RADIX)
                ]
                for p, pair in enumerate(radix_forward(chunks)):
                    for part, values in enumerate(pair):
                        h, w = split(values, 2)
                        at = slice(part * inner + start, part * inner + start + size)
                        high[p, here, at] = h
                        low[p, here, at] = w
            return carry

        lax.fori_loop(0, rows // 16, body, 0)

    p = pl.program_id(0)
    result = split_dot((high[p], low[p]), (table_ref[0, 0], table_ref[0, 1]), 1)
    for k in range(out_ref.shape[0]):
        out_ref[k] = result[:, k * piece : (k + 1) * piece]


def columns_kernel(planes, x_ref, table_ref, wave_ref, out_ref, high, low, rest, mixed, strips):
    length, width = x_ref.shape
    inner = length // RADIX
    pair_count = RADIX // 2
    step = pl.program_id(0)
    count, strip = strips.shape[0], strips.shape[1]

    @pl.when(step == 0)
    def _():
        def body(i, carry):
            for start, size in lane_slices(width):
                lanes = slice(start, start + size)
                chunks = [
                    x_ref[pl.ds(pl.multiple_of(l * inner + i * 16, 16), 16), lanes]
                    for l in range(RADIX)
                ]
                for p, pair in enumerate(radix_forward(chunks)):
                    for part, values in enumerate(pair):
                        h, w = split(values, 2)
                        here = pl.ds(pl.multiple_of(part * inner + i * 16, 16), 16)
                        high[p, here, lanes] = h
                        low[p, here, lanes] = w
            return carry

        lax.fori_loop(0, inner // 16, body, 0)

    @pl.when(step < pair_count)
    def _():
        p = step
        spectrum = split_dot((table_ref[0, 0], table_ref[0, 1]), (high[p], low[p]))
        row = lax.broadcasted_iota(jnp.int32, spectrum.shape, 0)
        second = jnp.where(p == 0, RADIX // 2, RADIX - p)
        index = jnp.where(row < inner, RADIX * row + p, RADIX * (row - inner) + second)
        folded = jnp.minimum(index, length - index).astype(jnp.float32)
        wave = (2.0 * math.pi / length) * folded
        column = wave_ref[...]
        screen = (2.0 * math.pi * screen_modes / length) ** 2
        denom = (wave * wave + column * column + screen) * float(length * length)
        factor = jnp.where((index == 0) & (column == 0.0), 0.0, -2.0 / denom)
        high[p], low[p], rest[p] = split(spectrum * factor, 3)

    @pl.when(step >= pair_count)
    def _():
        p = step - pair_count
        mixed[p] = split_dot(
            tuple(table_ref[0, k] for k in range(3)), (high[p], low[p], rest[p])
        )

    @pl.when(step == 2 * pair_count - 1)
    def _():
        per_chunk = inner // strip

        def body(i, carry):
            t = i * 16 // strip
            here = pl.ds(pl.multiple_of(i * 16 % strip, 16), 16)
            for start, size in lane_slices(width):
                lanes = slice(start, start + size)
                pairs = [
                    tuple(
                        mixed[p, pl.ds(pl.multiple_of(part * inner + i * 16, 16), 16), lanes]
                        for part in range(2)
                    )
                    for p in range(pair_count)
                ]
                for l, values in enumerate(radix_inverse(pairs)):
                    strips[l * per_chunk + t, here, lanes] = values
            return carry

        lax.fori_loop(0, inner // 16, body, 0)
        held = strip // STEP
        edge = MARGIN // STEP
        full = held + 2 * edge

        def assemble(t, carry):
            before = lax.rem(t + count - 1, count)
            after = lax.rem(t + 1, count)
            dest = lax.rem(t, planes) * (count // planes) + t // planes
            for m in range(STEP):
                base = m * full
                out_ref[dest, base : base + edge] = strips[
                    before, (m + 1) * held - edge : (m + 1) * held
                ]
                out_ref[dest, base + edge : base + edge + held] = strips[
                    t, m * held : (m + 1) * held
                ]
                out_ref[dest, base + edge + held : base + full] = strips[
                    after, m * held : m * held + edge
                ]
            return carry

        lax.fori_loop(0, count, assemble, 0)


def rows_inverse_kernel(x_ref, table_ref, out_ref, mixed):
    planes, pieces, rows, piece = x_ref.shape
    length = out_ref.shape[2]
    inner = length // RADIX
    p = pl.program_id(0)
    for plane in range(planes):
        total = None
        for k in range(pieces):
            at = slice(k * piece, (k + 1) * piece)
            term = split_dot(
                split(x_ref[plane, k], 3), tuple(table_ref[0, j, at, :] for j in range(3))
            )
            total = term if total is None else total + term
        mixed[plane, p] = total

    @pl.when(p == RADIX // 2 - 1)
    def _():
        for plane in range(planes):

            def body(i, carry):
                here = pl.ds(pl.multiple_of(i * 8, 8), 8)
                for start, size in lane_slices(inner):
                    pairs = [
                        tuple(
                            mixed[
                                plane, k, here, part * inner + start : part * inner + start + size
                            ]
                            for part in range(2)
                        )
                        for k in range(RADIX // 2)
                    ]
                    for l, values in enumerate(radix_inverse(pairs)):
                        out_ref[plane, here, l * inner + start : l * inner + start + size] = values
                return carry

            lax.fori_loop(0, rows // 8, body, 0)


def spline_terms(t):
    a = jnp.abs(t)
    p = jnp.maximum(2.0 - a, 0.0)
    q = jnp.maximum(1.0 - a, 0.0)
    p2 = p * p
    q2 = q * q
    weight = (p2 * p) * (1.0 / 6.0) - (q2 * q) * (2.0 / 3.0)
    slope = 2.0 * q2 - 0.5 * p2
    slope = jnp.where(t < 0.0, -slope, slope)
    return weight, slope, p - 4.0 * q


def rays_kernel(pot_ref, shift_ref, deflect_ref, jacob_ref, near, moved, down, first, total):
    rows, length = pot_ref.shape[1], pot_ref.shape[2]
    width = shift_ref.shape[2]
    groups = shift_ref.shape[1] // GROUP
    quota = rows // STEP
    centre = PATCH_ROWS // 2 - 1
    base_row = STEP // 2 - centre + MARGIN
    lane = lax.broadcasted_iota(jnp.int32, (rows, LANES), 1)

    def row_start(e, g):
        offset = base_row + centre + e
        return (offset % STEP) * quota + offset // STEP + GROUP * g

    def tile(s, carry):
        here = pl.ds(pl.multiple_of(s * LANES, LANES), LANES)
        origin = pl.program_id(0) * width + s * LANES

        def columns(plane, start):
            return pot_ref[plane, :, pl.ds(pl.multiple_of(start, LANES), LANES)]

        after = lax.rem(origin + LANES, length)
        before = lax.rem(origin + length - LANES, length)

        def shifted(plane, d):
            if isinstance(d, int) and d == 0:
                return columns(plane, origin)
            if isinstance(d, int):
                turn = -d % LANES
                other = after if d > 0 else before
            else:
                turn = lax.rem(2 * LANES - d, LANES)
                other = jnp.where(d >= 0, after, before)
            place = lane + d
            return jnp.where(
                (place >= 0) & (place < LANES),
                pltpu.roll(columns(plane, origin), turn, 1),
                pltpu.roll(columns(plane, other), turn, 1),
            )

        for k in range(5):
            near[k] = shifted(0, k - 2)

        bounds = None
        for g in range(groups):
            at = slice(g * GROUP, (g + 1) * GROUP)
            y = STEP * shift_ref[0, at, here]
            x = shift_ref[1, at, here]
            across = [spline_terms(x - float(k - 2)) for k in range(5)]
            sums = [None] * 5
            for e in range(-3, 4):
                r = row_start(e, g)
                cells = [near[k, r : r + GROUP, :] for k in range(5)]
                a0, a1, a2 = [
                    functools.reduce(
                        lambda u, v: u + v, [across[k][i] * cells[k] for k in range(5)]
                    )
                    for i in range(3)
                ]
                w, sl, cu = spline_terms(y - float(e))
                terms = (sl * a0, w * a1, cu * a0, w * a2, sl * a1)
                sums = [b if a is None else a + b for a, b in zip(sums, terms)]
            y2 = y - lens_ratio * sums[0]
            x2 = x - lens_ratio * sums[1]
            for k in range(5):
                first[g, k] = sums[k]
            first[g, 5] = y2
            first[g, 6] = x2
            mine = (y2, y2, x2, x2)
            if bounds is None:
                bounds = mine
            else:
                bounds = tuple(
                    jnp.minimum(a, b) if k % 2 == 0 else jnp.maximum(a, b)
                    for k, (a, b) in enumerate(zip(bounds, mine))
                )
        reach = float(2 * BLOCK)
        y_low = jnp.min(bounds[0])
        y_high = jnp.max(bounds[1])
        x_low = jnp.min(jnp.floor(jnp.clip(bounds[2], -reach, reach))).astype(jnp.int32)
        x_high = jnp.max(jnp.floor(jnp.clip(bounds[3], -reach, reach))).astype(jnp.int32)
        most = 2 * BLOCK - BLOCK // 2 - 1
        d_low = jnp.maximum(x_low - 1, -most)
        d_high = jnp.minimum(x_high + 2, most)

        def second(taps):
            for g in range(groups):
                y2 = first[g, 5]
                for e in taps:
                    w, sl, cu = spline_terms(y2 - float(e))
                    down[g, e + centre, 0] = w
                    down[g, e + centre, 1] = sl
                    down[g, e + centre, 2] = cu

            def column(d, c):
                cell = lax.rem(lane, BLOCK) + (BLOCK // 2) + d
                inside = (cell >= 0) & (cell < 2 * BLOCK)
                moved[...] = jnp.where(inside, shifted(1, d), 0.0)
                for g in range(groups):
                    b0 = b1 = b2 = None
                    for e in taps:
                        r = row_start(e, g)
                        cells = moved[r : r + GROUP, :]
                        t0 = down[g, e + centre, 0] * cells
                        t1 = down[g, e + centre, 1] * cells
                        t2 = down[g, e + centre, 2] * cells
                        b0 = t0 if b0 is None else b0 + t0
                        b1 = t1 if b1 is None else b1 + t1
                        b2 = t2 if b2 is None else b2 + t2
                    w, sl, cu = spline_terms(first[g, 6] - d.astype(jnp.float32))
                    terms = (w * b1, sl * b0, w * b2, cu * b0, sl * b1)
                    for k in range(5):
                        total[g, k] = total[g, k] + terms[k]
                return c

            lax.fori_loop(d_low, d_high + 1, column, 0)

        total[...] = jnp.zeros_like(total)
        narrow = (y_low >= -4.0) & (y_high <= 4.0)

        @pl.when(narrow)
        def _():
            second(range(-5, 6))

        @pl.when(jnp.logical_not(narrow))
        def _():
            second(range(-centre, PATCH_ROWS - centre))

        for g in range(groups):
            at = slice(g * GROUP, (g + 1) * GROUP)
            hess_yy, hess_xx, hess_xy = first[g, 2], first[g, 3], first[g, 4]
            other_yy, other_xx, other_xy = total[g, 2], total[g, 3], total[g, 4]
            lensed_yy = 1.0 - lens_ratio * hess_yy
            lensed_xx = 1.0 - lens_ratio * hess_xx
            lensed_xy = -lens_ratio * hess_xy
            deflect_ref[0, at, here] = first[g, 0] + total[g, 0]
            deflect_ref[1, at, here] = first[g, 1] + total[g, 1]
            jacob_ref[0, at, here] = (
                1.0 - hess_yy - (other_yy * lensed_yy + other_xy * lensed_xy)
            )
            jacob_ref[1, at, here] = -hess_xy - (other_yy * lensed_xy + other_xy * lensed_xx)
            jacob_ref[2, at, here] = -hess_xy - (other_xy * lensed_yy + other_xx * lensed_xy)
            jacob_ref[3, at, here] = (
                1.0 - hess_xx - (other_xy * lensed_xy + other_xx * lensed_xx)
            )
        return carry

    lax.fori_loop(0, width // LANES, tile, 0)


def params():
    return pltpu.CompilerParams(
        dimension_semantics=("arbitrary",), vmem_limit_bytes=56 * 1024 * 1024
    )


def on_device(tables, kappa, ray_offsets):
    rows, length = kappa.shape[1], kappa.shape[2]
    slabs = lax.axis_size("slab")
    planes = lax.axis_size("plane")
    strip = rows // planes
    padded = strip + 2 * MARGIN
    piece = length // slabs
    inner = length // RADIX
    pairs = RADIX // 2
    per_pair = 2 * inner // piece
    f32, bf16 = jnp.float32, jnp.bfloat16
    row_block = (1, 2, 2 * inner, 2 * inner)
    table_block = (1, 3, 2 * inner, 2 * inner)

    forward = pl.pallas_call(
        rows_forward_kernel,
        grid=(pairs,),
        in_specs=[
            pl.BlockSpec((rows, length), lambda i: (0, 0)),
            pl.BlockSpec(row_block, lambda i: (i, 0, 0, 0)),
        ],
        out_specs=pl.BlockSpec((per_pair, rows, piece), lambda i: (i, 0, 0)),
        out_shape=jax.ShapeDtypeStruct((slabs, rows, piece), f32),
        scratch_shapes=[pltpu.VMEM((pairs, rows, 2 * inner), bf16)] * 2,
        compiler_params=params(),
        name="rows_forward",
    )(kappa[0], tables)

    gathered = lax.all_to_all(forward, "slab", split_axis=0, concat_axis=0, tiled=True)

    position = lax.axis_index("slab") * piece + jnp.arange(piece, dtype=jnp.int32)
    pair = position // (2 * inner)
    half = position // inner % 2
    other = jnp.where(pair == 0, RADIX // 2, RADIX - pair)
    index = RADIX * (position % inner) + jnp.where(half == 0, pair, other)
    folded = jnp.minimum(index, length - index).astype(f32)
    wave = ((2.0 * math.pi / length) * folded)[None, :]

    strips = pl.pallas_call(
        functools.partial(columns_kernel, planes),
        grid=(2 * pairs,),
        in_specs=[
            pl.BlockSpec((length, piece), lambda i: (0, 0)),
            pl.BlockSpec(table_block, lambda i: (i, 0, 0, 0)),
            pl.BlockSpec((1, piece), lambda i: (0, 0)),
        ],
        out_specs=pl.BlockSpec((planes * slabs, padded, piece), lambda i: (0, 0, 0)),
        out_shape=jax.ShapeDtypeStruct((planes * slabs, padded, piece), f32),
        scratch_shapes=[
            pltpu.VMEM((pairs, 2 * inner, piece), bf16),
            pltpu.VMEM((pairs, 2 * inner, piece), bf16),
            pltpu.VMEM((pairs, 2 * inner, piece), bf16),
            pltpu.VMEM((pairs, 2 * inner, piece), f32),
            pltpu.VMEM((planes * slabs, strip, piece), f32),
        ],
        compiler_params=params(),
        name="columns",
    )(gathered.reshape(length, piece), tables, wave)

    arrived = lax.all_to_all(strips, ("plane", "slab"), split_axis=0, concat_axis=0, tiled=True)

    potential = pl.pallas_call(
        rows_inverse_kernel,
        grid=(pairs,),
        in_specs=[
            pl.BlockSpec((planes, per_pair, padded, piece), lambda i: (0, i, 0, 0)),
            pl.BlockSpec(table_block, lambda i: (i, 0, 0, 0)),
        ],
        out_specs=pl.BlockSpec((planes, padded, length), lambda i: (0, 0, 0)),
        out_shape=jax.ShapeDtypeStruct((planes, padded, length), f32),
        scratch_shapes=[pltpu.VMEM((planes, pairs, padded, 2 * inner), f32)],
        compiler_params=params(),
        name="rows_inverse",
    )(arrived.reshape(planes, slabs, padded, piece), tables)

    ray_rows = ray_offsets.shape[3]
    groups = ray_rows // GROUP
    width = min(4 * LANES, length)
    deflect, jacob = pl.pallas_call(
        rays_kernel,
        grid=(length // width,),
        in_specs=[
            pl.BlockSpec((planes, padded, length), lambda i: (0, 0, 0)),
            pl.BlockSpec((2, ray_rows, width), lambda i: (0, 0, i)),
        ],
        out_specs=[
            pl.BlockSpec((2, ray_rows, width), lambda i: (0, 0, i)),
            pl.BlockSpec((4, ray_rows, width), lambda i: (0, 0, i)),
        ],
        out_shape=[
            jax.ShapeDtypeStruct((2, ray_rows, length), f32),
            jax.ShapeDtypeStruct((4, ray_rows, length), f32),
        ],
        scratch_shapes=[
            pltpu.VMEM((5, padded, LANES), f32),
            pltpu.VMEM((padded, LANES), f32),
            pltpu.VMEM((groups, PATCH_ROWS, 3, GROUP, LANES), f32),
            pltpu.VMEM((groups, 7, GROUP, LANES), f32),
            pltpu.VMEM((groups, 5, GROUP, LANES), f32),
        ],
        compiler_params=params(),
        name="rays",
    )(potential, ray_offsets.reshape(2, ray_rows, length))
    return (deflect[:, None, None], jacob[:, None, None])


def solution(mesh):
    placed = (P("plane", "slab", None), P(None, "slab", "plane", None, None))

    def run(kappa, ray_offsets):
        length = kappa.shape[2]
        inner = length // RADIX
        strip = kappa.shape[1] // mesh.shape["slab"] // mesh.shape["plane"]
        tables = pair_tables(length)
        order = np.arange(inner).reshape(inner // strip, strip // STEP, STEP)
        order = order.transpose(0, 2, 1).reshape(-1)
        order = np.concatenate([order, order + inner])
        tables = split_table(
            np.concatenate([tables.transpose(0, 2, 1), tables[:, order, :]], axis=0), 3
        )
        body = functools.partial(on_device, jnp.asarray(tables))
        return jax.shard_map(
            body,
            mesh=mesh,
            in_specs=placed,
            out_specs=(P(None, "slab", "plane", None, None),) * 2,
            check_vma=False,
        )(kappa, ray_offsets)

    return run
```

time: 2320 us -> 324 us (0.14)
  matrix products: 1120 us -> 0 us
  local copies, waits for them, and re-layouts: 455 us -> 0 us
  other arithmetic: 351 us -> 0.59 us
  waiting for transfers between devices: 254 us -> 77.1 us
  blocking collectives: 0 us -> 126 us
  Pallas kernels: 0 us -> 111 us
  loops' own time: 79 us -> 0 us
  starting transfers between devices: 51.5 us -> 7.44 us
    dot_general x92 -> x0, matrix products: 1120 us -> none  [the longest x64 881 us: lens_fields(): jnp.einsum('pbc,bkrc->bkpr', plane_blocks, x_weights, precision=lax.Preci...]
    select_n x64 -> x0, other arithmetic: 189 us -> none  [spline_terms(): jnp.where(inside, 2.0 / 3.0 - magnitude * magnitude + 0.5 * magnitude * m...]
    all_to_all x4 -> x1, waiting for transfers between devices: 254 us -> 77.1 us  [on_device(): lax.all_to_all(forward, 'slab', split_axis=0, concat_axis=0, tiled=True)]
    all_to_all x0 -> x1, blocking collectives: none -> 126 us  [on_device(): lax.all_to_all(strips, ('plane', 'slab'), split_axis=0, concat_axis=0, ti...]
    dynamic_update_slice x128 -> x0, local copies, waits for them, and re-layouts: 120 us -> none  [on_device(): deflect, jacob = lax.map(one_row, jnp.arange(ray_count, dtype=jnp.int32))]
    reduce_sum x64 -> x0, other arithmetic: 120 us -> none  [lens_fields(): bend_down = jnp.sum(down_curves * across[:, 0], axis=1)]
    pallas_call x0 -> x4, Pallas kernels: none -> 111 us  [the longest x1 56.5 us: on_device(): pl.pallas_call(rays_kernel, grid=(length // width,), in_specs=[pl.BlockSp...]
    dynamic_slice x64 -> x0, local copies, waits for them, and re-layouts: 83.3 us -> none  [the longest x32 64.6 us: one_row(): window = lax.dynamic_slice_in_dim(padded, first_row, PATCH_ROWS, 1)]
  transfers between devices with their start and end apart: 4 -> 1, of which waited for: 4 -> 1; matrix products, arithmetic and copies ran while one was open for 5% -> 0% of each run, Pallas kernels for 0% -> 0%
where the time goes in v1:
time: 324 us; the launch traced here: 323 us
  blocking collectives  126 us (39%)
  Pallas kernels  111 us (34%)
  waiting for transfers between devices  77.1 us (24%)
  starting transfers between devices  7.44 us (2%)
    all_to_all x1, blocking collectives, on_device(): lax.all_to_all(strips, ('plane', 'slab'), split_axis=0, concat_axis=0, ti...  126 us
    all_to_all x1, waiting for transfers between devices, on_device(): lax.all_to_all(forward, 'slab', split_axis=0, concat_axis=0, tiled=True)  77.1 us
    pallas_call x1, Pallas kernels, on_device(): pl.pallas_call(rays_kernel, grid=(length // width,), in_specs=[pl.BlockSp...  56.5 us
    pallas_call x1, Pallas kernels, on_device(): pl.pallas_call(functools.partial(columns_kernel, planes), grid=(2 * pairs...  26.9 us
    pallas_call x1, Pallas kernels, on_device(): pl.pallas_call(rows_inverse_kernel, grid=(pairs,), in_specs=[pl.BlockSpec...  15.4 us
    pallas_call x1, Pallas kernels, on_device(): pl.pallas_call(rows_forward_kernel, grid=(pairs,), in_specs=[pl.BlockSpec...  12.5 us
    all_to_all x1, starting transfers between devices, on_device(): lax.all_to_all(forward, 'slab', split_axis=0, concat_axis=0, tiled=True)  7.44 us
  transfers between devices with their start and end apart: 1, of which 1 were waited for; matrix products, arithmetic and copies ran while one was open for 0% of the time, Pallas kernels for 0%

profile of v1, /device:TPU:0, one launch (start us, length us, event | category | flops | bytes accessed | tf_op | source)
XLA Modules:
  0.0 322.7 jit_solution(10496920170572355095)
XLA Ops:
  0.6 12.5 %rows_forward.1 = f32[16,256,256]{2,1,0:T(8,128)} custom-call(f32[256,4096]{1,0:T(8,128)} %bitcast.11, bf16[16,3,512,512]{3,2,1,0:T(8,128)(2,1)} %constant.63.clone.table_ref), custom_call_target="tpu_custom_call" | custom-call | tf_op jit(solution)/shard_map/rows_forward/pallas_call | solution.py:491
  13.2 7.4 %all-to-all-start = ((f32[16,256,256]{2,1,0:T(8,128)}), f32[16,256,256]{2,1,0:T(8,128)}, u32[]{:S(2)}, u32[]{:S(2)}) async-start(f32[16,256,256]{2,1,0:T(8,128)} %rows_forward.1), calls=%async_computation | async-start | bytes 8388608 | tf_op jit(solution)/shard_map/all_to_all | solution.py:505
  20.6 0.6 fusion.1.wave_ref
  21.2 77.1 %all-to-all-done = f32[16,256,256]{2,1,0:T(8,128)} async-done(((f32[16,256,256]{2,1,0:T(8,128)}), f32[16,256,256]{2,1,0:T(8,128)}, u32[]{:S(2)}, u32[]{:S(2)}) %all-to-all-start) | async-done | bytes 4194336 | tf_op jit(solution)/shard_map/all_to_all | solution.py:505
  98.3 26.9 %columns.1 = f32[32,144,256]{2,1,0:T(8,128)} custom-call(f32[4096,256]{1,0:T(8,128)} %bitcast.1.x_ref, bf16[16,3,512,512]{3,2,1,0:T(8,128)(2,1)} %constant.63.clone.table_ref, f32[1,256]{1,0:T(1,128)} %fusion.1.wave_ref), custom_call_target="tpu_custom_call" | custom-call | tf_op jit(solution)/shard_map/columns/pallas_call | solution.py:515
  125.2 125.6 %all_to_all.10 = f32[32,144,256]{2,1,0:T(8,128)} all-to-all(f32[32,144,256]{2,1,0:T(8,128)} %columns.1), channel_id=1, replica_groups=mesh['plane'=2,'slab'=16] {'plane','slab'}, dimensions={0} | all-to-all | bytes 9437184 | tf_op jit(solution)/shard_map/all_to_all | solution.py:536
  250.8 15.4 %rows_inverse.1.pot_ref = f32[2,144,4096]{2,1,0:T(8,128)} custom-call(f32[2,16,144,256]{3,2,1,0:T(8,128)} %bitcast.10, bf16[16,3,512,512]{3,2,1,0:T(8,128)(2,1)} %constant.63.clone.table_ref), custom_call_target="tpu_custom_call" | custom-call | tf_op jit(solution)/shard_map/rows_inverse/pallas_call | solution.py:538
  266.2 56.5 %rays.1 = (f32[2,32,4096]{2,1,0:T(8,128)}, f32[4,32,4096]{2,1,0:T(8,128)}) custom-call(f32[2,144,4096]{2,1,0:T(8,128)} %rows_inverse.1.pot_ref, f32[2,32,4096]{2,1,0:T(8,128)} %bitcast.12), custom_call_target="tpu_custom_call" | custom-call | tf_op jit(solution)/shard_map/rays/pallas_call | solution.py:555
Async XLA Ops:
  13.2 85.1 %all-to-all-start = ((f32[16,256,256]{2,1,0:T(8,128)}), f32[16,256,256]{2,1,0:T(8,128)}, u32[]{:S(2)}, u32[]{:S(2)}) async-start(f32[16,256,256]{2,1,0:T(8,128)} %rows_forward.1), calls=%async_computation | async-start | bytes 8388608 | tf_op jit(solution)/shard_map/all_to_all | solution.py:505
